TPU v7x, 1024 devices: a whole 8x8x8 slice. The times are simulated.
1024 devices in a mesh: fsdp: 32 (over x_lo, z, core), adapter: 32 (over x_hi, y).
Axes of the slice: x: 8 (x_hi: 4, x_lo: 2; x = x_hi * 2 + x_lo), y: 8, z: 8, core: 2. Of those that a mesh axis runs over, the one named last changes fastest.
Arguments:
- tokens: bfloat16 [131072, 6144], P(('fsdp', 'adapter')), may hold values from -6 to 6
- route_ids: int32 [131072, 2], P(('fsdp', 'adapter')), may hold values from 0 to 31, all different within a row; in each aligned block of 64 rows (0 to 63, 64 to 127, ...) at most 5 rows name the same one
- router_weight: bfloat16 [6144, 32], replicated, may hold values from -0.078125 to 0.078125
- adapter_down: bfloat16 [32, 6144, 32], P('adapter'), may hold values from -0.078125 to 0.078125
- adapter_up: bfloat16 [32, 32, 6144], P('adapter'), may hold values from -1 to 1
- norm_gain: float32 [6144], replicated, may hold values from 0.5 to 1.5
- frozen_weight: bfloat16 [6144, 512], P('fsdp'), may hold values from -0.078125 to 0.078125
Outputs:
- residual: bfloat16 [131072, 6144], P(('fsdp', 'adapter'))
- projected: bfloat16 [131072, 512], P(('fsdp', 'adapter'))
Inputs may be any that keep to these rules, and one draw needn't show every extreme that they name: `route_ids`: each row names two different adapter experts. Within each aligned block of 64 rows, no expert is named more than 5 times, a bound that some block reaches.
All inputs are finite; a program needn't handle non-finite values.
Results may differ from a plain program's by a relative error of at most 0.0056.
Values may be sent and summed in bfloat16 or wider, within the bound.
A program may use at most 64 MiB of HBM per device.

v0:
```python
import jax
import jax.numpy as jnp
from jax import lax
from jax.sharding import PartitionSpec as P


def shards(tokens, route_ids, router_weight, adapter_down, adapter_up, norm_gain, frozen_weight):
    rows = tokens.shape[0]
    half_rows = rows // 2
    width = tokens.shape[1]
    experts = router_weight.shape[1]
    per_owner = adapter_down.shape[0]
    capacity = max(2, 2 * half_rows // experts + 1)
    logits = jnp.dot(tokens, router_weight, preferred_element_type=jnp.float32)
    selector = route_ids[:, :, None] == jnp.arange(experts, dtype=jnp.int32)[None, None, :]
    chosen = jnp.sum(jnp.where(selector, logits[:, None, :], jnp.float32(0.0)), axis=2)
    leading = jax.nn.sigmoid(chosen[:, 0] - chosen[:, 1])
    gate_pair = jnp.stack([leading, 1.0 - leading], axis=1)
    pieces = []
    for round_number in range(2):
        lower = round_number * half_rows
        part_tokens = tokens[lower : lower + half_rows]
        part_ids = route_ids[lower : lower + half_rows]
        part_gate = gate_pair[lower : lower + half_rows]
        part_select = selector[lower : lower + half_rows]
        flat_ids = part_ids.reshape(-1)
        member = part_select.reshape(2 * half_rows, experts).astype(jnp.int32)
        earlier = jnp.cumsum(member, axis=0) - member
        slot_index = jnp.sum(earlier * member, axis=1)
        target = flat_ids * capacity + slot_index
        placing = (
            target[:, None] == jnp.arange(experts * capacity, dtype=jnp.int32)[None, :]
        ).astype(jnp.bfloat16)
        picking = jnp.sum(placing.reshape(half_rows, 2, experts * capacity), axis=1)
        outgoing = jnp.einsum("rs,rd->sd", picking, part_tokens, preferred_element_type=jnp.float32)
        outgoing = outgoing.astype(jnp.bfloat16).reshape(experts, capacity, width)
        received = lax.all_to_all(outgoing, "adapter", split_axis=0, concat_axis=0, tiled=True)
        sources = received.shape[0] // per_owner
        blocked = received.reshape(sources, per_owner, received.shape[1], width)
        low_rank = jnp.einsum(
            "secd,edr->secr", blocked, adapter_down, preferred_element_type=jnp.float32
        ).astype(jnp.bfloat16)
        answer = jnp.einsum(
            "secr,erd->secd", low_rank, adapter_up, preferred_element_type=jnp.float32
        ).astype(jnp.bfloat16)
        answer = answer.reshape(received.shape)
        returned_rows = lax.all_to_all(answer, "adapter", split_axis=0, concat_axis=0, tiled=True)
        flat_rows = returned_rows.reshape(experts * capacity, width)
        fetched = jnp.take(flat_rows, target, axis=0).reshape(half_rows, 2, width)
        first_term = part_gate[:, 0:1] * fetched[:, 0, :].astype(jnp.float32)
        second_term = part_gate[:, 1:2] * fetched[:, 1, :].astype(jnp.float32)
        pieces.append(first_term + second_term)
    summed = jnp.concatenate(pieces, axis=0)
    combined = tokens.astype(jnp.float32) + summed
    residual = combined.astype(jnp.bfloat16)
    scale = lax.rsqrt(jnp.mean(combined * combined, axis=1, keepdims=True) + 1e-05)
    normed = (combined * scale * norm_gain[None, :]).astype(jnp.bfloat16)
    projected = jnp.dot(
        normed,
        lax.all_gather(frozen_weight, "fsdp", axis=0, tiled=True),
        preferred_element_type=jnp.float32,
    )
    return (residual, projected.astype(jnp.bfloat16))


def solution(mesh):
    return jax.shard_map(
        shards,
        mesh=mesh,
        in_specs=(
            P(("fsdp", "adapter"), None),
            P(("fsdp", "adapter"), None),
            P(),
            P("adapter", None, None),
            P("adapter", None, None),
            P(),
            P("fsdp", None),
        ),
        out_specs=(P(("fsdp", "adapter"), None), P(("fsdp", "adapter"), None)),
        check_vma=False,
    )
```

profile of v0, /device:TPU:386, one launch (start us, length us, event | category | flops | bytes accessed | tf_op | source)
XLA Modules:
  0.0 535.9 jit_solution(16495729806595772812)
XLA Ops:
  8.7 2.2 fusion.31
  12.6 1.8 convolution_convert_fusion.1
  14.4 2.5 reshape.131
  17.0 12.0 %all-to-all-start.2 = ((bf16[32,5,6144]{2,1,0:T(8,128)(2,1)}), bf16[32,5,6144]{2,1,0:T(8,128)(2,1)S(1)}, u32[]{:S(2)}, u32[]{:S(2)}) async-start(bf16[32,5,6144]{2,1,0:T(8,128)(2,1)} %reshape.131), calls=%async_computation.2 | async-start | bytes 6291456 | tf_op jit(solution)/shard_map/all_to_all | solution.py:37
  28.9 3.1 convolution_convert_fusion.3
  32.1 4.3 reshape.126
  36.4 79.7 %all-to-all-done.2 = bf16[32,5,6144]{2,1,0:T(8,128)(2,1)S(1)} async-done(((bf16[32,5,6144]{2,1,0:T(8,128)(2,1)}), bf16[32,5,6144]{2,1,0:T(8,128)(2,1)S(1)}, u32[]{:S(2)}, u32[]{:S(2)}) %all-to-all-start.2) | async-done | bytes 1966112 | tf_op jit(solution)/shard_map/all_to_all | solution.py:37
  116.1 12.0 %all-to-all-start = ((bf16[32,5,6144]{2,1,0:T(8,128)(2,1)}), bf16[32,5,6144]{2,1,0:T(8,128)(2,1)}, u32[]{:S(2)}, u32[]{:S(2)}) async-start(bf16[32,5,6144]{2,1,0:T(8,128)(2,1)} %reshape.126), calls=%async_computation | async-start | bytes 6291456 | tf_op jit(solution)/shard_map/all_to_all | solution.py:37
  128.1 4.8 convolution_convert_fusion
  132.9 4.3 copy.100
  137.2 73.9 %all-to-all-done = bf16[32,5,6144]{2,1,0:T(8,128)(2,1)} async-done(((bf16[32,5,6144]{2,1,0:T(8,128)(2,1)}), bf16[32,5,6144]{2,1,0:T(8,128)(2,1)}, u32[]{:S(2)}, u32[]{:S(2)}) %all-to-all-start) | async-done | bytes 1966112 | tf_op jit(solution)/shard_map/all_to_all | solution.py:37
  211.1 57.9 %all-to-all-start.3 = ((bf16[32,5,6144]{2,1,0:T(8,128)(2,1)}), bf16[32,5,6144]{2,1,0:T(8,128)(2,1)S(1)}, u32[]{:S(2)}, u32[]{:S(2)}) async-start(bf16[32,5,6144]{2,1,0:T(8,128)(2,1)} %copy.100), calls=%async_computation.3 | async-start | bytes 6291456 | tf_op jit(solution)/shard_map/all_to_all | solution.py:47
  269.7 5.8 %convolution_convert_fusion.2 = bf16[32,5,6144]{2,0,1:T(8,128)(2,1)} fusion(bf16[32,5,6144]{2,1,0:T(8,128)(2,1)} %all-to-all-done, bf16[1,32,6144]{2,1,0:T(8,128)(2,1)S(1)} %copy-done, bf16[1,6144,32]{1,2,0:T(8,128)(2,1)} %param.12), kind=kOutput, calls=%fused_computation.4 | convolution fusion | flops 126817280 | bytes 4718592 | tf_op jit(solution)/shard_map/secr,erd->secd/dot_general | solution.py:43
  275.4 4.4 copy.94
  279.8 85.7 %all-to-all-done.3 = bf16[32,5,6144]{2,1,0:T(8,128)(2,1)S(1)} async-done(((bf16[32,5,6144]{2,1,0:T(8,128)(2,1)}), bf16[32,5,6144]{2,1,0:T(8,128)(2,1)S(1)}, u32[]{:S(2)}, u32[]{:S(2)}) %all-to-all-start.3) | async-done | bytes 1966112 | tf_op jit(solution)/shard_map/all_to_all | solution.py:47
  365.6 43.5 %all-to-all-start.1 = ((bf16[32,5,6144]{2,1,0:T(8,128)(2,1)}), bf16[32,5,6144]{2,1,0:T(8,128)(2,1)}, u32[]{:S(2)}, u32[]{:S(2)}) async-start(bf16[32,5,6144]{2,1,0:T(8,128)(2,1)} %copy.94), calls=%async_computation.1 | async-start | bytes 6291456 | tf_op jit(solution)/shard_map/all_to_all | solution.py:47
  409.6 2.0 fusion.43
  413.9 3.0 reshape.132
  416.9 1.5 gather_fusion.1
  418.4 0.9 broadcast_select_fusion
  419.3 1.0 reshape.133
  420.3 82.5 %all-to-all-done.1 = bf16[32,5,6144]{2,1,0:T(8,128)(2,1)} async-done(((bf16[32,5,6144]{2,1,0:T(8,128)(2,1)}), bf16[32,5,6144]{2,1,0:T(8,128)(2,1)}, u32[]{:S(2)}, u32[]{:S(2)}) %all-to-all-start.1) | async-done | bytes 1966112 | tf_op jit(solution)/shard_map/all_to_all | solution.py:47
  502.9 3.0 reshape.129
  505.9 2.6 gather_fusion
  508.5 2.8 broadcast_select_fusion.1
  511.3 3.4 reshape.130
  514.7 2.2 fusion.42
  517.0 1.2 fusion.5
  518.2 2.2 fusion.41
  520.5 1.2 fusion.6
  521.9 1.7 multiply_reduce_fusion
  523.6 5.5 %fusion.9 = bf16[128,512]{1,0:T(8,128)(2,1)} fusion(bf16[6144,512]{1,0:T(8,128)(2,1)} %all-gather.2.cloned.1.call-done, f32[6144]{0:T(1024)S(1)} %copy-done.10, f32[128]{0:T(128)S(1)} %add_rsqrt_fusion, f32[64,6144]{1,0:T(8,128)S(1)} %fusion.5, f32[64,6144]{1,0:T(8,128)} %copy-done.3, bf16[128,6144]{1,0:T(8,128)(2,1)} %param.9), kind=kOutput, calls=%fused_computation.24 | convolution fusion | flops 810090496 | bytes 11166208 | tf_op jit(solution)/shard_map/dot_general | solution.py:58
  (48 shorter events, 6.8 us)
Async XLA Ops:
  7.2 120.9 %copy-start = (bf16[1,32,6144]{2,1,0:T(8,128)(2,1)S(1)}, bf16[1,32,6144]{2,1,0:T(8,128)(2,1)}, u32[]{:S(2)}) copy-start(bf16[1,32,6144]{2,1,0:T(8,128)(2,1)} %param.13) | copy-start | bytes 1179652
  8.0 4.6 copy-start.5
  17.0 99.1 %all-to-all-start.2 = ((bf16[32,5,6144]{2,1,0:T(8,128)(2,1)}), bf16[32,5,6144]{2,1,0:T(8,128)(2,1)S(1)}, u32[]{:S(2)}, u32[]{:S(2)}) async-start(bf16[32,5,6144]{2,1,0:T(8,128)(2,1)} %reshape.131), calls=%async_computation.2 | async-start | bytes 6291456 | tf_op jit(solution)/shard_map/all_to_all | solution.py:37
  116.1 95.0 %all-to-all-start = ((bf16[32,5,6144]{2,1,0:T(8,128)(2,1)}), bf16[32,5,6144]{2,1,0:T(8,128)(2,1)}, u32[]{:S(2)}, u32[]{:S(2)}) async-start(bf16[32,5,6144]{2,1,0:T(8,128)(2,1)} %reshape.126), calls=%async_computation | async-start | bytes 6291456 | tf_op jit(solution)/shard_map/all_to_all | solution.py:37
  211.1 154.5 %all-to-all-start.3 = ((bf16[32,5,6144]{2,1,0:T(8,128)(2,1)}), bf16[32,5,6144]{2,1,0:T(8,128)(2,1)S(1)}, u32[]{:S(2)}, u32[]{:S(2)}) async-start(bf16[32,5,6144]{2,1,0:T(8,128)(2,1)} %copy.100), calls=%async_computation.3 | async-start | bytes 6291456 | tf_op jit(solution)/shard_map/all_to_all | solution.py:47
  269.0 254.6 %all-gather.2.cloned.1.call-start = ((), (), s32[]{:S(2)}) async-start(), calls=%async_computation.4 | async-start | bytes 6488064 | tf_op jit(solution)/shard_map/all_gather | solution.py:60
  365.6 47.8 %copy-start.2 = (bf16[32,5,6144]{2,1,0:T(8,128)(2,1)}, bf16[32,5,6144]{2,1,0:T(8,128)(2,1)S(1)}, u32[]{:S(2)}) copy-start(bf16[32,5,6144]{2,1,0:T(8,128)(2,1)S(1)} %all-to-all-done.3) | copy-start | bytes 5898244
  365.6 137.3 %all-to-all-start.1 = ((bf16[32,5,6144]{2,1,0:T(8,128)(2,1)}), bf16[32,5,6144]{2,1,0:T(8,128)(2,1)}, u32[]{:S(2)}, u32[]{:S(2)}) async-start(bf16[32,5,6144]{2,1,0:T(8,128)(2,1)} %copy.94), calls=%async_computation.1 | async-start | bytes 6291456 | tf_op jit(solution)/shard_map/all_to_all | solution.py:47
  409.1 2.6 copy-start.6
  505.9 2.6 copy-start.9
  514.7 2.3 copy-start.7
  514.7 2.3 copy-start.8
  520.4 1.4 copy-start.4
  521.9 1.7 copy-start.3
  521.9 1.7 copy-start.10
  523.6 5.5 %copy-start.1 = (bf16[1,32,6144]{2,1,0:T(8,128)(2,1)S(1)}, bf16[1,32,6144]{2,1,0:T(8,128)(2,1)}, u32[]{:S(2)}) copy-start(bf16[1,32,6144]{2,1,0:T(8,128)(2,1)} %param.13) | copy-start | bytes 1179652
Sparse Core Ops, SparseCore 0:
  272.5 94.9 all-gather.1
where the time goes:
time: 537 us; the launch traced here: 536 us
  waiting for transfers between devices  322 us (60%)
  starting transfers between devices  126 us (23%)
  local copies, waits for them, and re-layouts  37 us (7%)
  matrix products  23 us (4%)
  between operations  14.3 us (3%)
  other arithmetic  13.6 us (3%)
    all_to_all x2, waiting for transfers between devices, shards(): lax.all_to_all(answer, 'adapter', split_axis=0, concat_axis=0, tiled=True)  168 us
    all_to_all x2, waiting for transfers between devices, shards(): lax.all_to_all(outgoing, 'adapter', split_axis=0, concat_axis=0, tiled=True)  154 us
    all_to_all x2, starting transfers between devices, shards(): lax.all_to_all(answer, 'adapter', split_axis=0, concat_axis=0, tiled=True)  101 us
    all_to_all x2, starting transfers between devices, shards(): lax.all_to_all(outgoing, 'adapter', split_axis=0, concat_axis=0, tiled=True)  24 us
  transfers between devices with their start and end apart: 5, of which 4 were waited for; matrix products, arithmetic and copies ran while one was open for 11% of the time, Pallas kernels for 0%

commit v1 on v0

v1 whole, which is shorter than its diff:
```python
import functools

import jax
import jax.numpy as jnp
from jax import lax
from jax.experimental import pallas as pl
from jax.experimental.pallas import tpu as pltpu
from jax.sharding import PartitionSpec as P

MESH = pl.DeviceIdType.MESH
NX, NY, NZ = 8, 8, 8
CHAINS = ((0, 1, 4), (1, 1, 3), (0, -1, 3), (1, -1, 4))
CHUNK = 256


def mult(value, of):
    return pl.multiple_of(value, of)


def flip(bit, by):
    return bit + by * (1 - 2 * bit)


def kernel(
    tok, code, down, up, router, frozen, gain, res, proj,
    X, CODE, DN, UP, RT, FZ, ACC0, ACC1, ACCR, P1, PIN, TS, TIN, A, RB, PB, PIN2,
    tok_s, tok_r, code_s, code_r, xd_s, xd_r, xu_s, xu_r, yd_s, yd_r, yu_s, yu_r,
    fz_s, fz_r, p1_s, p1_r, t_s, t_r, rb_s, rb_r, p2_s, p2_r, rt_sem,
):
    half = tok.shape[0] // 2
    width = X.shape[1]
    rank = down.shape[0]
    block = 4 * rank
    per_class = width // frozen.shape[0]
    fs, ad = lax.axis_index("fsdp"), lax.axis_index("adapter")
    x_lo = lax.div(fs, 2 * NZ)
    z = lax.rem(lax.div(fs, 2), NZ)
    core = lax.rem(fs, 2)
    x_hi = lax.div(ad, NY)
    y = lax.rem(ad, NY)
    x = 2 * x_hi + x_lo
    zb = lax.rem(z, 2)
    mine = x_lo * 4 + zb * 2 + core

    def dev(px, py, pz, pc):
        return (lax.rem(px, 2) * (2 * NZ) + pz * 2 + pc, lax.div(px, 2) * NY + py)

    def partner(h, d):
        px, pz, pc = x, z, core
        if d & 4:
            px = x + 1 - 2 * x_lo if h == 0 else lax.rem(x + NX - 1 + 2 * x_lo, NX)
        if d & 2:
            pz = z + 1 - 2 * zb if h == 0 else lax.rem(z + NZ - 1 + 2 * zb, NZ)
        if d & 1:
            pc = 1 - core
        return dev(px, y, pz, pc)

    def member(d):
        return flip(x_lo, (d >> 2) & 1) * 4 + flip(zb, (d >> 1) & 1) * 2 + flip(core, d & 1)

    own_cols = pl.ds(mult(mine * width, 128), width)
    groups = [(h, d) for d in (6, 4, 2, 7, 5, 3, 1) for h in range(2)]

    def remote(src, dst, send, recv, device):
        return pltpu.make_async_remote_copy(
            src_ref=src, dst_ref=dst, send_sem=send, recv_sem=recv, device_id=device, device_id_type=MESH
        )

    def rows_of(h, d):
        return pl.ds((h * 8 + d) * half, half)

    def tok_copy(h, d):
        i = h * 8 + d
        cols = pl.ds(mult(member(d) * width, 128), width)
        src = tok.at[pl.ds(h * half, half), cols]
        return remote(src, X.at[rows_of(h, d)], tok_s.at[i], tok_r.at[i], partner(h, d))

    def code_copy(h, d):
        i = h * 8 + d
        src = code.at[pl.ds(h * half, half)]
        return remote(src, CODE.at[rows_of(h, d)], code_s.at[i], code_r.at[i], partner(h, d))

    def slot(py, px_hi):
        return pl.ds(mult(py * block + px_hi * rank, rank), rank)

    def x_copy(src, buf, send, recv, d):
        device = dev(2 * lax.rem(x_hi + d, 4) + x_lo, y, z, core)
        return remote(src.at[:, own_cols], buf.at[slot(y, x_hi)], send.at[d], recv.at[d], device)

    def y_copy(buf, send, recv, chain, s):
        part, way, _ = CHAINS[chain]
        origin = lax.rem(y + NY - way * (s - 1), NY)
        rows = pl.ds(mult(origin * block + part * (block // 2), block // 2), block // 2)
        device = dev(x, lax.rem(y + NY + way, NY), z, core)
        i = chain * 4 + s - 1
        return remote(buf.at[rows], buf.at[rows], send.at[i], recv.at[i], device)

    fz_class = lax.div(fs, per_class)
    fz_core = lax.rem(fz_class, 2)
    fz_zb = lax.rem(lax.div(fz_class, 2), 2)
    fz_rows = frozen.shape[0]
    fz_slot = pl.ds(mult(lax.rem(fs, per_class) * fz_rows, 16), fz_rows)
    fz_self = (fz_class == mine)

    def fz_dest(k):
        return dev(x, y, 2 * k + fz_zb, fz_core)

    def fz_other(k):
        return jnp.logical_not(jnp.logical_and(2 * k + fz_zb == z, fz_core == core))

    def fz_copy(k):
        return remote(frozen, FZ.at[fz_slot], fz_s.at[k], fz_r.at[lax.rem(fs, per_class)], fz_dest(k))

    barrier = pltpu.get_barrier_semaphore()

    def greet(device):
        pl.semaphore_signal(barrier, inc=1, device_id=device, device_id_type=MESH)

    for h, d in groups:
        greet(partner(h, d))
    for d in range(1, 4):
        greet(dev(2 * lax.rem(x_hi + d, 4) + x_lo, y, z, core))
    for way in (1, -1):
        greet(dev(x, lax.rem(y + NY + way, NY), z, core))
    for b in range(per_class):
        source = mine * per_class + b

        @pl.when(source != fs)
        def _():
            greet((source, ad))

    RT[...] = jnp.zeros_like(RT)
    pl.semaphore_wait(barrier, 14 + 3 + 2 + NZ // 2 - fz_self.astype(jnp.int32))

    for src, buf, send, recv in ((down, DN, xd_s, xd_r),):
        for d in (2, 1, 3):
            x_copy(src, buf, send, recv, d).start()
        pltpu.make_async_copy(src.at[:, own_cols], buf.at[slot(y, x_hi)], recv.at[0]).start()
    for h, d in groups:
        code_copy(h, d).start()
        tok_copy(h, d).start()

    def tok_local(h):
        cp = pltpu.make_async_copy(tok.at[pl.ds(h * half, half), own_cols], X.at[rows_of(h, 0)], tok_r.at[h * 8])
        cq = pltpu.make_async_copy(code.at[pl.ds(h * half, half)], CODE.at[rows_of(h, 0)], code_r.at[h * 8])
        return cp, cq

    for h in range(2):
        for c in tok_local(h):
            c.start()
    rt_copy = pltpu.make_async_copy(router.at[:, own_cols], RT.at[pl.ds(2 * rank, rank)], rt_sem.at[0])
    rt_copy.start()

    def x_wait(src, buf, send, recv):
        pltpu.make_async_copy(src.at[:, own_cols], buf.at[slot(y, x_hi)], recv.at[0]).wait()
        for d in (1, 3, 2):
            x_copy(src, buf, send, recv, d).wait_recv()

    x_wait(down, DN, xd_s, xd_r)
    for c in range(4):
        y_copy(DN, yd_s, yd_r, c, 1).start()
    for d in (2, 1, 3):
        x_copy(up, UP, xu_s, xu_r, d).start()
    pltpu.make_async_copy(up.at[:, own_cols], UP.at[slot(y, x_hi)], xu_r.at[0]).start()

    for h in range(2):
        for c in tok_local(h):
            c.wait()
    for h, d in groups:
        code_copy(h, d).wait_recv()
        tok_copy(h, d).wait_recv()
    rt_copy.wait()

    total = X.shape[0]
    lane = lax.broadcasted_iota(jnp.int32, (CHUNK, 128), 1)
    group8 = (lane >> 5) * 8
    nt = (((1,), (1,)), ((), ()))

    def low_rank(py, first=False):
        def body(i, carry):
            rows = pl.ds(mult(i * CHUNK, CHUNK), CHUNK)
            xs = X[rows, :]
            got = lax.dot_general(
                xs, DN[pl.ds(mult(py * block, block), block), :], nt, preferred_element_type=jnp.float32
            )
            c = CODE[rows, :]
            id0, id1 = c >> 5, c & 31
            named = group8 + py
            part0 = jnp.where(id0 == named, got, 0.0)
            part1 = jnp.where(id1 == named, got, 0.0)
            if first:
                ACC0[rows, :] = part0
                ACC1[rows, :] = part1
                logit = lax.dot_general(xs, RT[...], nt, preferred_element_type=jnp.float32)
                at = lane - 64
                ACCR[rows, :] = jnp.where(at == id0, logit, 0.0) - jnp.where(at == id1, logit, 0.0)
            else:
                ACC0[rows, :] += part0
                ACC1[rows, :] += part1
            return carry

        lax.fori_loop(0, total // CHUNK, body, 0)

    def ring_step(buf, send, recv, s):
        for c in (0, 3, 1, 2):
            if s <= CHAINS[c][2]:
                y_copy(buf, send, recv, c, s).wait_recv()
                if s < CHAINS[c][2]:
                    y_copy(buf, send, recv, c, s + 1).start()

    low_rank(y, True)
    for s in range(1, 5):
        ring_step(DN, yd_s, yd_r, s)
        if s == 1:
            for k in range(NZ // 2):
                @pl.when(fz_other(k))
                def _():
                    fz_copy(k).start()

            @pl.when(fz_self)
            def _():
                pltpu.make_async_copy(frozen, FZ.at[fz_slot], fz_r.at[lax.rem(fs, per_class)]).start()
        if s == 3:
            x_wait(up, UP, xu_s, xu_r)
            for c in range(4):
                y_copy(UP, yu_s, yu_r, c, 1).start()
        low_rank(lax.rem(y + NY - s, NY))
        if s < 4:
            low_rank(lax.rem(y + s, NY))

    def pack(i, carry):
        rows = pl.ds(mult(i * CHUNK, CHUNK), CHUNK)
        a0, a1 = ACC0[rows, :], ACC1[rows, :]
        a0 = a0 + pltpu.roll(a0, 64, 1)
        a0 = a0 + pltpu.roll(a0, 32, 1)
        a1 = a1 + pltpu.roll(a1, 64, 1)
        a1 = a1 + pltpu.roll(a1, 32, 1)
        low = jnp.where(lane < 32, a0, a1)
        P1[rows, :] = jnp.where(lane < 64, low, jnp.where(lane < 96, ACCR[rows, :], 0.0))
        return carry

    lax.fori_loop(0, total // CHUNK, pack, 0)

    def p1_copy(h, d):
        i = h * 8 + d
        return remote(P1.at[rows_of(h, d)], PIN.at[rows_of(h, d)], p1_s.at[i], p1_r.at[i], partner(h, d))

    for h, d in groups:
        p1_copy(h, d).start()
    ring_step(UP, yu_s, yu_r, 1)
    for h, d in groups:
        p1_copy(h, d).wait_recv()

    def t_copy(h, d):
        i = h * 8 + d
        return remote(TS.at[pl.ds(h * half, half)], TIN.at[rows_of(h, d)], t_s.at[i], t_r.at[i], partner(h, d))

    lane_h = lax.broadcasted_iota(jnp.int32, (half, 128), 1)
    for h in range(2):
        s = P1[rows_of(h, 0), :]
        for d in range(1, 8):
            s = s + PIN[rows_of(h, d), :]
        rounded = s.astype(jnp.bfloat16).astype(jnp.float32)
        t0 = jnp.where(lane_h < 32, rounded, 0.0)
        t1 = jnp.where(jnp.logical_and(lane_h >= 32, lane_h < 64), rounded, 0.0)
        t0 = t0 + pltpu.roll(t0, 32, 1)
        t0 = t0 + pltpu.roll(t0, 64, 1)
        t1 = t1 + pltpu.roll(t1, 32, 1)
        t1 = t1 + pltpu.roll(t1, 64, 1)
        gap = jnp.sum(jnp.where(lane_h >= 64, s, 0.0), axis=1, keepdims=True)
        g0 = jax.nn.sigmoid(gap)
        pair = jnp.concatenate([g0 * t0, (1.0 - g0) * t1], axis=1).astype(jnp.bfloat16)
        TS[pl.ds(h * half, half), :] = pair
        TIN[rows_of(h, 0), :] = pair
        for hh, d in groups:
            if hh == h:
                t_copy(h, d).start()

    ring_step(UP, yu_s, yu_r, 2)
    for h, d in groups:
        t_copy(h, d).wait_recv()

    def spread(i, carry):
        rows = pl.ds(mult(i * CHUNK, CHUNK), CHUNK)
        c = CODE[rows, :]
        id0, id1 = c >> 5, c & 31
        t0 = TIN[rows, 0:128].astype(jnp.float32)
        t1 = TIN[rows, 128:256].astype(jnp.float32)
        for py in range(NY):
            named = group8 + py
            part = jnp.where(id0 == named, t0, jnp.where(id1 == named, t1, 0.0))
            A[rows, py * block : (py + 1) * block] = part.astype(jnp.bfloat16)
        return carry

    lax.fori_loop(0, total // CHUNK, spread, 0)
    ring_step(UP, yu_s, yu_r, 3)
    for b in range(per_class):
        into = FZ.at[pl.ds(b * fz_rows, fz_rows)]
        pltpu.make_async_copy(frozen, into, fz_r.at[b]).wait()
    ring_step(UP, yu_s, yu_r, 4)

    def rb_copy(h, d):
        i = h * 8 + d
        dst = res.at[pl.ds(h * half, half), own_cols]
        return remote(RB.at[rows_of(h, d)], dst, rb_s.at[i], rb_r.at[i], partner(h, d))

    def rb_local(h):
        dst = res.at[pl.ds(h * half, half), own_cols]
        return pltpu.make_async_copy(RB.at[rows_of(h, 0)], dst, rb_r.at[h * 8])

    def p2_copy(h, d):
        i = h * 8 + d
        return remote(PB.at[rows_of(h, d)], PIN2.at[rows_of(h, d)], p2_s.at[i], p2_r.at[i], partner(h, d))

    features = proj.shape[1]
    for i in (1, 3, 0, 2):
        rows = pl.ds(i * CHUNK, CHUNK)
        delta = jnp.dot(A[rows, :], UP[...], preferred_element_type=jnp.float32)
        combined = X[rows, :].astype(jnp.float32) + delta
        RB[rows, :] = combined.astype(jnp.bfloat16)
        blocks = range(i * (CHUNK // 64), (i + 1) * (CHUNK // 64))
        for k in reversed(blocks):
            if k % 8:
                rb_copy(k // 8, k % 8).start()
            else:
                rb_local(k // 8).start()
        square = combined * combined
        lanes = square[:, 0:128]
        for j in range(1, width // 128):
            lanes = lanes + square[:, j * 128 : (j + 1) * 128]
        scaled = (combined * gain[:, own_cols]).astype(jnp.bfloat16)
        part = jnp.dot(scaled, FZ[...], preferred_element_type=jnp.float32)
        PB[rows, 0:features] = part.astype(jnp.bfloat16)
        PB[rows, features : features + 128] = lanes.astype(jnp.bfloat16)
        for k in reversed(blocks):
            if k % 8:
                p2_copy(k // 8, k % 8).start()

    for h in range(2):
        for hh, d in groups:
            if hh == h:
                p2_copy(h, d).wait_recv()
        s = PB[rows_of(h, 0), :].astype(jnp.float32)
        for d in range(1, 8):
            s = s + PIN2[rows_of(h, d), :].astype(jnp.float32)
        mean = jnp.sum(s[:, features:], axis=1, keepdims=True) / tok.shape[1]
        proj[pl.ds(h * half, half), :] = (s[:, :features] * lax.rsqrt(mean + 1e-05)).astype(jnp.bfloat16)

    for h in range(2):
        rb_local(h).wait()
    for h, d in groups:
        rb_copy(h, d).wait_recv()
        for copy in (tok_copy, code_copy, p1_copy, t_copy, rb_copy, p2_copy):
            copy(h, d).wait_send()
    for d in range(1, 4):
        x_copy(down, DN, xd_s, xd_r, d).wait_send()
        x_copy(up, UP, xu_s, xu_r, d).wait_send()
    for c in range(4):
        for s in range(1, CHAINS[c][2] + 1):
            y_copy(DN, yd_s, yd_r, c, s).wait_send()
            y_copy(UP, yu_s, yu_r, c, s).wait_send()
    for k in range(NZ // 2):
        @pl.when(fz_other(k))
        def _():
            fz_copy(k).wait_send()


def shards(tokens, route_ids, router_weight, adapter_down, adapter_up, norm_gain, frozen_weight):
    rows, width = tokens.shape
    part = width // 8
    features = frozen_weight.shape[1]
    total = 8 * rows
    code = jnp.broadcast_to((route_ids[:, 0] * 32 + route_ids[:, 1])[:, None], (rows, 128))
    bf, f32 = jnp.bfloat16, jnp.float32
    dma = pltpu.SemaphoreType.DMA
    any_spec = pl.BlockSpec(memory_space=pl.ANY)
    vmem = pl.BlockSpec(memory_space=pltpu.VMEM)
    sems = [16] * 4 + [4] * 4 + [16] * 4 + [4] * 2 + [16] * 8 + [1]
    return pl.pallas_call(
        kernel,
        out_shape=(
            jax.ShapeDtypeStruct((rows, width), bf),
            jax.ShapeDtypeStruct((rows, features), bf),
        ),
        in_specs=[any_spec] * 6 + [vmem],
        out_specs=(any_spec, vmem),
        scratch_shapes=[
            pltpu.VMEM((total, part), bf),
            pltpu.VMEM((total, 128), jnp.int32),
            pltpu.VMEM((1024, part), bf),
            pltpu.VMEM((1024, part), bf),
            pltpu.VMEM((128, part), bf),
            pltpu.VMEM((part, features), bf),
            pltpu.VMEM((total, 128), f32),
            pltpu.VMEM((total, 128), f32),
            pltpu.VMEM((total, 128), f32),
            pltpu.VMEM((total, 128), f32),
            pltpu.VMEM((total, 128), f32),
            pltpu.VMEM((rows, 256), bf),
            pltpu.VMEM((total, 256), bf),
            pltpu.VMEM((total, 1024), bf),
            pltpu.VMEM((total, part), bf),
            pltpu.VMEM((total, features + 128), bf),
            pltpu.VMEM((total, features + 128), bf),
        ]
        + [dma((n,)) for n in sems],
        compiler_params=pltpu.CompilerParams(
            collective_id=0, has_side_effects=True, vmem_limit_bytes=48 * 1024 * 1024
        ),
        cost_estimate=pl.CostEstimate(flops=6_000_000_000, bytes_accessed=20_000_000, transcendentals=0),
    )(
        tokens,
        code,
        jnp.swapaxes(adapter_down[0], 0, 1),
        adapter_up[0],
        jnp.swapaxes(router_weight, 0, 1),
        frozen_weight,
        norm_gain[None, :],
    )


def solution(mesh):
    return jax.shard_map(
        shards,
        mesh=mesh,
        in_specs=(
            P(("fsdp", "adapter"), None),
            P(("fsdp", "adapter"), None),
            P(),
            P("adapter", None, None),
            P("adapter", None, None),
            P(),
            P("fsdp", None),
        ),
        out_specs=(P(("fsdp", "adapter"), None), P(("fsdp", "adapter"), None)),
        check_vma=False,
    )
```

time: 537 us -> 112 us (0.21)
  the two profiles are of different devices: /device:TPU:386 before, /device:TPU:131 now
where the time goes in v1:
time: 112 us
  Pallas kernels  103 us (92%)
  local copies, waits for them, and re-layouts  7.94 us (7%)
    pallas_call x1, Pallas kernels, shards(): pl.pallas_call(kernel, out_shape=(jax.ShapeDtypeStruct((rows, width), bf)...  103 us
    unnamed x14, local copies, waits for them, and re-layouts  7.86 us

profile of v1, /device:TPU:131, one launch (start us, length us, event | category | flops | bytes accessed | tf_op | source)
XLA Modules:
  0.0 111.9 jit_solution(8108147793681366155)
XLA Ops:
  0.6 0.8 add_bitcast_fusion
  1.4 0.1 broadcast_in_dim.12.code
  1.5 0.0 copy-start
  1.5 1.4 %copy-done = bf16[128,6144]{1,0:T(8,128)(2,1)S(1)} copy-done((bf16[128,6144]{1,0:T(8,128)(2,1)S(1)}, bf16[128,6144]{1,0:T(8,128)(2,1)}, u32[]{:S(2)}) %copy-start) | copy-done | bytes 1572888
  2.9 0.0 copy-start.1
  2.9 1.0 copy-done.1
  3.9 0.0 copy-start.2
  3.9 1.0 copy-done.2
  4.9 0.0 copy-start.3
  4.9 1.0 copy-done.3
  5.9 0.0 copy-start.4
  5.9 0.9 copy-done.4
  6.8 0.0 copy-start.5
  6.8 0.7 copy-done.5
  7.5 102.5 %shard_map.86 = (bf16[128,6144]{1,0:T(8,128)(2,1)S(1)}, bf16[128,512]{1,0:T(8,128)(2,1)S(1)}) custom-call(bf16[128,6144]{1,0:T(8,128)(2,1)S(1)} %copy-done, s32[128,128]{1,0:T(8,128)S(1)} %broadcast_in_dim.12.code, bf16[32,6144]{1,0:T(8,128)(2,1)S(1)} %bitcast.8, bf16[32,6144]{1,0:T(8,128)(2,1)S(1)} %bitcast.9, bf16[32,6144]{1,0:T(8,128)(2,1)S(1)} %bitcast.10, ...), custom_call_target="tpu_custom_call" | custom-call | flops 6000000000 | bytes 20000000 | tf_op jit(solution)/shard_map/pallas_call | solution.py:379
  110.1 1.1 %copy.11 = bf16[128,6144]{1,0:T(8,128)(2,1)} copy(bf16[128,6144]{1,0:T(8,128)(2,1)S(1)} %get-tuple-element.4) | data formatting | bytes 3145728
  111.2 0.7 copy.12
Async XLA Ops:
  1.5 1.4 %copy-start = (bf16[128,6144]{1,0:T(8,128)(2,1)S(1)}, bf16[128,6144]{1,0:T(8,128)(2,1)}, u32[]{:S(2)}) copy-start(bf16[128,6144]{1,0:T(8,128)(2,1)} %tok.1) | copy-start | bytes 4718596
  2.9 1.0 copy-start.1
  3.9 1.0 copy-start.2
  4.9 1.0 copy-start.3
  5.9 0.9 copy-start.4
  6.8 0.7 copy-start.5

commit v2 on v1

v2 whole, which is shorter than its diff:
```python
import functools

import jax
import jax.numpy as jnp
from jax import lax
from jax.experimental import pallas as pl
from jax.experimental.pallas import tpu as pltpu
from jax.sharding import PartitionSpec as P

MESH = pl.DeviceIdType.MESH
NX, NY, NZ = 8, 8, 8
CHUNK = 256


def mult(value, of):
    return pl.multiple_of(value, of)


def flip(bit, by):
    return bit + by * (1 - 2 * bit)


def kernel(
    tok, ids, down, up, router, frozen, gain, res, proj,
    X, IDS, CODE, DN, UP, RT, FZ, ACC0, ACC1, ACCR, P1, PIN, TS, TIN, A, RB, PB, PS, PO, PIN2,
    tok_s, tok_r, id_s, id_r, xd_s, xd_r, xu_s, xu_r, yd_s, yd_r, yu_s, yu_r,
    fz_s, fz_r, p1_s, p1_r, t_s, t_r, rb_s, rb_r, ps_s, ps_r, p2_s, p2_r, rt_sem,
):
    half = tok.shape[0] // 2
    width = X.shape[1]
    total = X.shape[0]
    rank = down.shape[0]
    block = 4 * rank
    features = proj.shape[1]
    per_class = width // frozen.shape[0]
    fs, ad = lax.axis_index("fsdp"), lax.axis_index("adapter")
    x_lo = lax.div(fs, 2 * NZ)
    z = lax.rem(lax.div(fs, 2), NZ)
    core = lax.rem(fs, 2)
    x_hi = lax.div(ad, NY)
    y = lax.rem(ad, NY)
    x = 2 * x_hi + x_lo
    zb = lax.rem(z, 2)
    mine = x_lo * 4 + zb * 2 + core

    def dev(px, py, pz, pc):
        return (lax.rem(px, 2) * (2 * NZ) + pz * 2 + pc, lax.div(px, 2) * NY + py)

    def partner(h, d):
        px, pz, pc = x, z, core
        if d & 4:
            px = x + 1 - 2 * x_lo if h == 0 else lax.rem(x + NX - 1 + 2 * x_lo, NX)
        if d & 2:
            pz = z + 1 - 2 * zb if h == 0 else lax.rem(z + NZ - 1 + 2 * zb, NZ)
        if d & 1:
            pc = 1 - core
        return dev(px, y, pz, pc)

    def member(d):
        return flip(x_lo, (d >> 2) & 1) * 4 + flip(zb, (d >> 1) & 1) * 2 + flip(core, d & 1)

    def cols_of(m):
        return pl.ds(mult(m * width, 128), width)

    own_cols = cols_of(mine)
    x_groups = [(h, d) for d in (6, 4, 7, 5) for h in range(2)]
    z_groups = [(h, d) for d in (2, 3, 1) for h in range(2)]
    groups = x_groups + z_groups

    def remote(src, dst, send, recv, device):
        return pltpu.make_async_remote_copy(
            src_ref=src, dst_ref=dst, send_sem=send, recv_sem=recv, device_id=device, device_id_type=MESH
        )

    def rows_of(h, d):
        return pl.ds((h * 8 + d) * half, half)

    def tok_copy(h, d):
        i = h * 8 + d
        src = tok.at[pl.ds(h * half, half), cols_of(member(d))]
        return remote(src, X.at[rows_of(h, d)], tok_s.at[i], tok_r.at[i], partner(h, d))

    def id_copy(h, d):
        i = h * 8 + d
        return remote(ids, IDS.at[i], id_s.at[i], id_r.at[i], partner(h, d))

    def tok_local(h):
        cp = pltpu.make_async_copy(tok.at[pl.ds(h * half, half), own_cols], X.at[rows_of(h, 0)], tok_r.at[h * 8])
        cq = pltpu.make_async_copy(ids, IDS.at[h * 8], id_r.at[h * 8])
        return cp, cq

    def slot(py, px_hi):
        return pl.ds(mult(py * block + px_hi * rank, rank), rank)

    def x_copy(src, buf, send, recv, i):
        px = lax.rem(x + (2 * x_lo - 1) * i + NX, NX)
        cols = cols_of(lax.rem(px, 2) * 4 + zb * 2 + core)
        return remote(src.at[:, cols], buf.at[slot(y, x_hi)], send.at[i], recv.at[i], dev(px, y, z, core))

    def x_source(i):
        return lax.rem(x + (1 - 2 * x_lo) * (-i if i % 2 else i) + NX, NX)

    def x_local(src, buf, recv):
        return pltpu.make_async_copy(src.at[:, own_cols], buf.at[slot(y, x_hi)], recv.at[0])

    def steps(q, way):
        return 4 if (q < 2) == (way == 1) else 3

    def y_copy(buf, send, recv, q, way, s):
        origin = lax.rem(y + NY - way * (s - 1), NY)
        rows = slot(origin, lax.div(x_source(q), 2) if q else x_hi)
        device = dev(x, lax.rem(y + NY + way, NY), z, core)
        i = (q * 2 + (way + 1) // 2) * 4 + s - 1
        return remote(buf.at[rows], buf.at[rows], send.at[i], recv.at[i], device)

    def ring_start(buf, send, recv, q):
        for way in (1, -1):
            y_copy(buf, send, recv, q, way, 1).start()

    def ring_step(buf, send, recv, s):
        for q in range(4):
            for way in (1, -1):
                if s <= steps(q, way):
                    y_copy(buf, send, recv, q, way, s).wait_recv()
                    if s < steps(q, way):
                        y_copy(buf, send, recv, q, way, s + 1).start()

    fz_class = lax.div(fs, per_class)
    fz_core = lax.rem(fz_class, 2)
    fz_zb = lax.rem(lax.div(fz_class, 2), 2)
    fz_rows = frozen.shape[0]
    fz_slot = pl.ds(mult(lax.rem(fs, per_class) * fz_rows, 16), fz_rows)
    fz_self = fz_class == mine

    def fz_other(k):
        return jnp.logical_not(jnp.logical_and(2 * k + fz_zb == z, fz_core == core))

    def fz_copy(k):
        device = dev(x, y, 2 * k + fz_zb, fz_core)
        return remote(frozen, FZ.at[fz_slot], fz_s.at[k], fz_r.at[lax.rem(fs, per_class)], device)

    barrier = pltpu.get_barrier_semaphore()

    def greet(device):
        pl.semaphore_signal(barrier, inc=1, device_id=device, device_id_type=MESH)

    for i in range(1, 4):
        greet(dev(x_source(i), y, z, core))
    for way in (1, -1):
        greet(dev(x, lax.rem(y + NY + way, NY), z, core))
    for h, d in groups:
        greet(partner(h, d))
    for b in range(per_class):
        source = mine * per_class + b

        @pl.when(source != fs)
        def _():
            greet((source, ad))

    x_local(down, DN, xd_r).start()
    x_local(up, UP, xu_r).start()
    RT[...] = jnp.zeros_like(RT)
    rt_copy = pltpu.make_async_copy(router.at[:, own_cols], RT.at[pl.ds(2 * rank, rank)], rt_sem.at[0])
    rt_copy.start()
    for h in range(2):
        for c in tok_local(h):
            c.start()
    pl.semaphore_wait(barrier, 14 + 3 + 2 + NZ // 2 - fz_self.astype(jnp.int32))

    for i in range(1, 4):
        x_copy(down, DN, xd_s, xd_r, i).start()
    x_local(down, DN, xd_r).wait()
    ring_start(DN, yd_s, yd_r, 0)
    for h, d in groups:
        id_copy(h, d).start()
    for h, d in z_groups:
        tok_copy(h, d).start()

    for i in range(1, 4):
        x_copy(down, DN, xd_s, xd_r, i).wait_recv()
        ring_start(DN, yd_s, yd_r, i)
    for h, d in x_groups:
        tok_copy(h, d).start()
    for i in range(1, 4):
        x_copy(up, UP, xu_s, xu_r, i).start()

    ring_step(DN, yd_s, yd_r, 1)
    ring_step(DN, yd_s, yd_r, 2)

    for h in range(2):
        for c in tok_local(h):
            c.wait()
    for h, d in groups:
        id_copy(h, d).wait_recv()
    for h in range(2):
        for d in range(8):
            pair = IDS[h * 8 + d]
            both = (pair[0:1, :] * 32 + pair[1:2, :]).astype(jnp.float32)
            spread_out = jnp.transpose(jnp.broadcast_to(both, (128, 128)))
            CODE[rows_of(h, d), :] = spread_out[h * half : (h + 1) * half, :].astype(jnp.int32)
    for h, d in z_groups + x_groups:
        tok_copy(h, d).wait_recv()
    rt_copy.wait()
    for k in range(NZ // 2):
        @pl.when(fz_other(k))
        def _():
            fz_copy(k).start()

    @pl.when(fz_self)
    def _():
        pltpu.make_async_copy(frozen, FZ.at[fz_slot], fz_r.at[lax.rem(fs, per_class)]).start()

    lane = lax.broadcasted_iota(jnp.int32, (CHUNK, 128), 1)
    group8 = (lane >> 5) * 8
    nt = (((1,), (1,)), ((), ()))

    def low_rank(py, first=False):
        def body(i, carry):
            rows = pl.ds(mult(i * CHUNK, CHUNK), CHUNK)
            xs = X[rows, :]
            got = lax.dot_general(
                xs, DN[pl.ds(mult(py * block, block), block), :], nt, preferred_element_type=jnp.float32
            )
            c = CODE[rows, :]
            id0, id1 = c >> 5, c & 31
            named = group8 + py
            part0 = jnp.where(id0 == named, got, 0.0)
            part1 = jnp.where(id1 == named, got, 0.0)
            if first:
                ACC0[rows, :] = part0
                ACC1[rows, :] = part1
                logit = lax.dot_general(xs, RT[...], nt, preferred_element_type=jnp.float32)
                at = lane - 64
                ACCR[rows, :] = jnp.where(at == id0, logit, 0.0) - jnp.where(at == id1, logit, 0.0)
            else:
                ACC0[rows, :] += part0
                ACC1[rows, :] += part1
            return carry

        lax.fori_loop(0, total // CHUNK, body, 0)

    low_rank(y, True)
    ring_step(DN, yd_s, yd_r, 3)
    x_local(up, UP, xu_r).wait()
    ring_start(UP, yu_s, yu_r, 0)
    for i in range(1, 4):
        x_copy(up, UP, xu_s, xu_r, i).wait_recv()
        ring_start(UP, yu_s, yu_r, i)
    for s in (1, 2):
        low_rank(lax.rem(y + NY - s, NY))
        low_rank(lax.rem(y + s, NY))
    ring_step(DN, yd_s, yd_r, 4)
    low_rank(lax.rem(y + NY - 3, NY))
    low_rank(lax.rem(y + 3, NY))
    low_rank(lax.rem(y + 4, NY))

    def pack(i, carry):
        rows = pl.ds(mult(i * CHUNK, CHUNK), CHUNK)
        a0, a1 = ACC0[rows, :], ACC1[rows, :]
        a0 = a0 + pltpu.roll(a0, 64, 1)
        a0 = a0 + pltpu.roll(a0, 32, 1)
        a1 = a1 + pltpu.roll(a1, 64, 1)
        a1 = a1 + pltpu.roll(a1, 32, 1)
        low = jnp.where(lane < 32, a0, a1)
        P1[rows, :] = jnp.where(lane < 64, low, jnp.where(lane < 96, ACCR[rows, :], 0.0))
        return carry

    lax.fori_loop(0, total // CHUNK, pack, 0)

    def p1_copy(h, d):
        i = h * 8 + d
        return remote(P1.at[rows_of(h, d)], PIN.at[rows_of(h, d)], p1_s.at[i], p1_r.at[i], partner(h, d))

    for h, d in groups:
        p1_copy(h, d).start()
    ring_step(UP, yu_s, yu_r, 1)
    for h, d in groups:
        p1_copy(h, d).wait_recv()

    def t_copy(h, d):
        i = h * 8 + d
        return remote(TS.at[pl.ds(h * half, half)], TIN.at[rows_of(h, d)], t_s.at[i], t_r.at[i], partner(h, d))

    lane_h = lax.broadcasted_iota(jnp.int32, (half, 128), 1)
    for h in range(2):
        s = P1[rows_of(h, 0), :]
        for d in range(1, 8):
            s = s + PIN[rows_of(h, d), :]
        rounded = s.astype(jnp.bfloat16).astype(jnp.float32)
        gap = jnp.sum(jnp.where(lane_h >= 64, s, 0.0), axis=1, keepdims=True)
        g0 = jax.nn.sigmoid(gap)
        gated = rounded * jnp.where(lane_h < 32, g0, 1.0 - g0)
        pair = jnp.where(lane_h < 64, gated, 0.0).astype(jnp.bfloat16)
        TS[pl.ds(h * half, half), :] = pair
        TIN[rows_of(h, 0), :] = pair
        for hh, d in groups:
            if hh == h:
                t_copy(h, d).start()

    ring_step(UP, yu_s, yu_r, 2)
    for h, d in groups:
        t_copy(h, d).wait_recv()

    def spread(i, carry):
        rows = pl.ds(mult(i * CHUNK, CHUNK), CHUNK)
        c = CODE[rows, :]
        id0, id1 = c >> 5, c & 31
        t = TIN[rows, :].astype(jnp.float32)
        t0 = jnp.where(lane < 32, t, 0.0)
        t1 = t - t0
        t0 = t0 + pltpu.roll(t0, 32, 1)
        t0 = t0 + pltpu.roll(t0, 64, 1)
        t1 = t1 + pltpu.roll(t1, 32, 1)
        t1 = t1 + pltpu.roll(t1, 64, 1)
        for py in range(NY):
            named = group8 + py
            part = jnp.where(id0 == named, t0, jnp.where(id1 == named, t1, 0.0))
            A[rows, py * block : (py + 1) * block] = part.astype(jnp.bfloat16)
        return carry

    lax.fori_loop(0, total // CHUNK, spread, 0)
    ring_step(UP, yu_s, yu_r, 3)
    for b in range(per_class):
        into = FZ.at[pl.ds(b * fz_rows, fz_rows)]
        pltpu.make_async_copy(frozen, into, fz_r.at[b]).wait()
    ring_step(UP, yu_s, yu_r, 4)

    def rb_copy(h, d):
        i = h * 8 + d
        dst = res.at[pl.ds(h * half, half), own_cols]
        return remote(RB.at[rows_of(h, d)], dst, rb_s.at[i], rb_r.at[i], partner(h, d))

    def rb_local(h):
        dst = res.at[pl.ds(h * half, half), own_cols]
        return pltpu.make_async_copy(RB.at[rows_of(h, 0)], dst, rb_r.at[h * 8])

    def ps_copy(h, d):
        i = h * 8 + d
        return remote(PB.at[rows_of(h, d)], PS.at[rows_of(h, d - 1)], ps_s.at[i], ps_r.at[i], partner(0, 1))

    def p2_copy(h, d):
        i = h * 8 + d
        return remote(PO.at[rows_of(h, d)], PIN2.at[rows_of(h, d)], p2_s.at[i], p2_r.at[i], partner(h, d))

    for i in (1, 3, 0, 2):
        rows = pl.ds(i * CHUNK, CHUNK)
        delta = jnp.dot(A[rows, :], UP[...], preferred_element_type=jnp.float32)
        combined = X[rows, :].astype(jnp.float32) + delta
        RB[rows, :] = combined.astype(jnp.bfloat16)
        blocks = [(4 * i + k) for k in (2, 0, 3, 1)]
        for k in blocks:
            if k % 8:
                rb_copy(k // 8, k % 8).start()
            else:
                rb_local(k // 8).start()
        square = combined * combined
        lanes = square[:, 0:128]
        for j in range(1, width // 128):
            lanes = lanes + square[:, j * 128 : (j + 1) * 128]
        scaled = (combined * gain[:, own_cols]).astype(jnp.bfloat16)
        PB[rows, 0:features] = jnp.dot(scaled, FZ[...], preferred_element_type=jnp.float32)
        PB[rows, features : features + 128] = lanes
        for k in blocks:
            if k % 2:
                ps_copy(k // 8, k % 8).start()

    for d in (6, 4, 2):
        for h in range(2):
            ps_copy(h, d + 1).wait_recv()
            rows = rows_of(h, d)
            PO[rows, :] = (PB[rows, :] + PS[rows, :]).astype(jnp.bfloat16)
            p2_copy(h, d).start()

    for h in range(2):
        ps_copy(h, 1).wait_recv()
        s = PB[rows_of(h, 0), :] + PS[rows_of(h, 0), :]
        for d in (6, 4, 2):
            p2_copy(h, d).wait_recv()
            s = s + PIN2[rows_of(h, d), :].astype(jnp.float32)
        mean = jnp.sum(s[:, features:], axis=1, keepdims=True) / tok.shape[1]
        proj[pl.ds(h * half, half), :] = (s[:, :features] * lax.rsqrt(mean + 1e-05)).astype(jnp.bfloat16)

    for h in range(2):
        rb_local(h).wait()
    for h, d in groups:
        rb_copy(h, d).wait_recv()
        for copy in (tok_copy, id_copy, p1_copy, t_copy, rb_copy):
            copy(h, d).wait_send()
    for h in range(2):
        for d in (1, 3, 5, 7):
            ps_copy(h, d).wait_send()
        for d in (2, 4, 6):
            p2_copy(h, d).wait_send()
    for i in range(1, 4):
        x_copy(down, DN, xd_s, xd_r, i).wait_send()
        x_copy(up, UP, xu_s, xu_r, i).wait_send()
    for q in range(4):
        for way in (1, -1):
            for s in range(1, steps(q, way) + 1):
                y_copy(DN, yd_s, yd_r, q, way, s).wait_send()
                y_copy(UP, yu_s, yu_r, q, way, s).wait_send()
    for k in range(NZ // 2):
        @pl.when(fz_other(k))
        def _():
            fz_copy(k).wait_send()


def shards(tokens, route_ids, router_weight, adapter_down, adapter_up, norm_gain, frozen_weight):
    rows, width = tokens.shape
    part = width // 8
    features = frozen_weight.shape[1]
    total = 8 * rows
    bf, f32 = jnp.bfloat16, jnp.float32
    dma = pltpu.SemaphoreType.DMA
    any_spec = pl.BlockSpec(memory_space=pltpu.HBM)
    vmem = pl.BlockSpec(memory_space=pltpu.VMEM)
    sems = [16] * 4 + [4] * 4 + [32] * 4 + [4] * 2 + [16] * 10 + [1]
    return pl.pallas_call(
        kernel,
        out_shape=(
            jax.ShapeDtypeStruct((rows, width), bf),
            jax.ShapeDtypeStruct((rows, features), bf),
        ),
        in_specs=[any_spec] * 6 + [vmem],
        out_specs=(any_spec, vmem),
        scratch_shapes=[
            pltpu.VMEM((total, part), bf),
            pltpu.VMEM((16, 2, rows), jnp.int32),
            pltpu.VMEM((total, 128), jnp.int32),
            pltpu.VMEM((1024, part), bf),
            pltpu.VMEM((1024, part), bf),
            pltpu.VMEM((128, part), bf),
            pltpu.VMEM((part, features), bf),
            pltpu.VMEM((total, 128), f32),
            pltpu.VMEM((total, 128), f32),
            pltpu.VMEM((total, 128), f32),
            pltpu.VMEM((total, 128), f32),
            pltpu.VMEM((total, 128), f32),
            pltpu.VMEM((rows, 128), bf),
            pltpu.VMEM((total, 128), bf),
            pltpu.VMEM((total, 1024), bf),
            pltpu.VMEM((total, part), bf),
            pltpu.VMEM((total, features + 128), f32),
            pltpu.VMEM((total, features + 128), f32),
            pltpu.VMEM((total, features + 128), bf),
            pltpu.VMEM((total, features + 128), bf),
        ]
        + [dma((n,)) for n in sems],
        compiler_params=pltpu.CompilerParams(
            collective_id=0, has_side_effects=True, vmem_limit_bytes=60 * 1024 * 1024
        ),
        cost_estimate=pl.CostEstimate(flops=6_000_000_000, bytes_accessed=20_000_000, transcendentals=0),
    )(
        tokens,
        jnp.swapaxes(route_ids, 0, 1),
        jnp.swapaxes(adapter_down[0], 0, 1),
        adapter_up[0],
        jnp.swapaxes(router_weight, 0, 1),
        frozen_weight,
        norm_gain[None, :],
    )


def solution(mesh):
    return jax.shard_map(
        shards,
        mesh=mesh,
        in_specs=(
            P(("fsdp", "adapter"), None),
            P(("fsdp", "adapter"), None),
            P(),
            P("adapter", None, None),
            P("adapter", None, None),
            P(),
            P("fsdp", None),
        ),
        out_specs=(P(("fsdp", "adapter"), None), P(("fsdp", "adapter"), None)),
        check_vma=False,
    )
```

time: 112 us -> 103 us (0.920)
  the two profiles are of different devices: /device:TPU:131 before, /device:TPU:128 now
where the time goes in v2:
time: 103 us
  Pallas kernels  98.5 us (96%)
  local copies, waits for them, and re-layouts  3.38 us (3%)
    pallas_call x1, Pallas kernels, shards(): pl.pallas_call(kernel, out_shape=(jax.ShapeDtypeStruct((rows, width), bf)...  98.5 us
    unnamed x4, local copies, waits for them, and re-layouts  3.38 us

profile of v2, /device:TPU:128, one launch (start us, length us, event | category | flops | bytes accessed | tf_op | source)
XLA Modules:
  0.0 102.6 jit_solution(7568905516262653913)
XLA Ops:
  0.6 98.5 %shard_map.86 = (bf16[128,6144]{1,0:T(8,128)(2,1)}, bf16[128,512]{1,0:T(8,128)(2,1)}) custom-call(bf16[128,6144]{1,0:T(8,128)(2,1)} %tok.1, s32[2,128]{1,0:T(2,128)} %bitcast.11, bf16[32,6144]{1,0:T(8,128)(2,1)} %bitcast.7, bf16[32,6144]{1,0:T(8,128)(2,1)} %bitcast.8, bf16[32,6144]{1,0:T(8,128)(2,1)} %bitcast.9, bf16[192,512]{1,0:T(8,128)(2,1)} %frozen.1, ...), custom_call_target="tpu_custom_call" | custom-call | flops 6000000000 | bytes 20000000 | tf_op jit(solution)/shard_map/pallas_call | solution.py:418
  99.2 0.0 copy-start
  99.2 2.7 %copy.11 = bf16[128,6144]{1,0:T(8,128)(2,1)} copy(bf16[128,6144]{1,0:T(8,128)(2,1)} %get-tuple-element.4) | data formatting | bytes 3145728
  101.9 0.0 copy-done
  101.9 0.7 copy.12
Async XLA Ops:
  99.2 2.7 %copy-start = (bf16[128,512]{1,0:T(8,128)(2,1)S(1)}, bf16[128,512]{1,0:T(8,128)(2,1)}, u32[]{:S(2)}) copy-start(bf16[128,512]{1,0:T(8,128)(2,1)} %get-tuple-element.5) | copy-start | bytes 393220

commit v3 on v2

--- a/solution.py
+++ b/solution.py
@@ -22,7 +22,7 @@
 
 def kernel(
     tok, ids, down, up, router, frozen, gain, res, proj,
-    X, IDS, CODE, DN, UP, RT, FZ, ACC0, ACC1, ACCR, P1, PIN, TS, TIN, A, RB, PB, PS, PO, PIN2,
+    X, IDS, CODE, DN, UP, RT, FZ, ACC0, ACC1, ACCR, P1, PIN, TS, TIN, A, RB, PB, PS, PO, PIN2, GAIN,
     tok_s, tok_r, id_s, id_r, xd_s, xd_r, xu_s, xu_r, yd_s, yd_r, yu_s, yu_r,
     fz_s, fz_r, p1_s, p1_r, t_s, t_r, rb_s, rb_r, ps_s, ps_r, p2_s, p2_r, rt_sem,
 ):
@@ -162,6 +162,8 @@
     RT[...] = jnp.zeros_like(RT)
     rt_copy = pltpu.make_async_copy(router.at[:, own_cols], RT.at[pl.ds(2 * rank, rank)], rt_sem.at[0])
     rt_copy.start()
+    gain_copy = pltpu.make_async_copy(gain.at[:, own_cols], GAIN, rt_sem.at[1])
+    gain_copy.start()
     for h in range(2):
         for c in tok_local(h):
             c.start()
@@ -181,38 +183,40 @@
         ring_start(DN, yd_s, yd_r, i)
     for h, d in x_groups:
         tok_copy(h, d).start()
-    for i in range(1, 4):
-        x_copy(up, UP, xu_s, xu_r, i).start()
-
-    ring_step(DN, yd_s, yd_r, 1)
-    ring_step(DN, yd_s, yd_r, 2)
-
-    for h in range(2):
-        for c in tok_local(h):
-            c.wait()
-    for h, d in groups:
-        id_copy(h, d).wait_recv()
-    for h in range(2):
-        for d in range(8):
-            pair = IDS[h * 8 + d]
-            both = (pair[0:1, :] * 32 + pair[1:2, :]).astype(jnp.float32)
-            spread_out = jnp.transpose(jnp.broadcast_to(both, (128, 128)))
-            CODE[rows_of(h, d), :] = spread_out[h * half : (h + 1) * half, :].astype(jnp.int32)
-    for h, d in z_groups + x_groups:
-        tok_copy(h, d).wait_recv()
-    rt_copy.wait()
-    for k in range(NZ // 2):
-        @pl.when(fz_other(k))
-        def _():
-            fz_copy(k).start()
-
-    @pl.when(fz_self)
-    def _():
-        pltpu.make_async_copy(frozen, FZ.at[fz_slot], fz_r.at[lax.rem(fs, per_class)]).start()
 
     lane = lax.broadcasted_iota(jnp.int32, (CHUNK, 128), 1)
     group8 = (lane >> 5) * 8
     nt = (((1,), (1,)), ((), ()))
+
+    def take_ids():
+        for h in range(2):
+            tok_local(h)[1].wait()
+        for h, d in groups:
+            id_copy(h, d).wait_recv()
+        for h in range(2):
+            for d in range(8):
+                pair = IDS[h * 8 + d]
+                both = (pair[0:1, :] * 32 + pair[1:2, :]).astype(jnp.float32)
+                down_rows = jnp.transpose(jnp.broadcast_to(both, (128, 128)))
+                CODE[rows_of(h, d), :] = down_rows[h * half : (h + 1) * half, :].astype(jnp.int32)
+
+    def take_tokens():
+        for h in range(2):
+            tok_local(h)[0].wait()
+        for h, d in z_groups + x_groups:
+            tok_copy(h, d).wait_recv()
+        rt_copy.wait()
+        gain_copy.wait()
+
+    def send_frozen():
+        for k in range(NZ // 2):
+            @pl.when(fz_other(k))
+            def _():
+                fz_copy(k).start()
+
+        @pl.when(fz_self)
+        def _():
+            pltpu.make_async_copy(frozen, FZ.at[fz_slot], fz_r.at[lax.rem(fs, per_class)]).start()
 
     def low_rank(py, first=False):
         def body(i, carry):
@@ -239,91 +243,119 @@
 
         lax.fori_loop(0, total // CHUNK, body, 0)
 
+    def low_rank_at(s):
+        low_rank(lax.rem(y + NY - s, NY))
+        if s < 4:
+            low_rank(lax.rem(y + s, NY))
+
+    def p1_copy(h, d):
+        i = h * 8 + d
+        return remote(P1.at[rows_of(h, d)], PIN.at[rows_of(h, d)], p1_s.at[i], p1_r.at[i], partner(h, d))
+
+    def send_partials():
+        def pack(i, carry):
+            rows = pl.ds(mult(i * CHUNK, CHUNK), CHUNK)
+            a0, a1 = ACC0[rows, :], ACC1[rows, :]
+            a0 = a0 + pltpu.roll(a0, 64, 1)
+            a0 = a0 + pltpu.roll(a0, 32, 1)
+            a1 = a1 + pltpu.roll(a1, 64, 1)
+            a1 = a1 + pltpu.roll(a1, 32, 1)
+            low = jnp.where(lane < 32, a0, a1)
+            P1[rows, :] = jnp.where(lane < 64, low, jnp.where(lane < 96, ACCR[rows, :], 0.0))
+            return carry
+
+        lax.fori_loop(0, total // CHUNK, pack, 0)
+        for h, d in groups:
+            p1_copy(h, d).start()
+
+    def t_copy(h, d):
+        i = h * 8 + d
+        return remote(TS.at[pl.ds(h * half, half)], TIN.at[rows_of(h, d)], t_s.at[i], t_r.at[i], partner(h, d))
+
+    def send_gated():
+        lane_h = lax.broadcasted_iota(jnp.int32, (half, 128), 1)
+        for h in range(2):
+            for hh, d in groups:
+                if hh == h:
+                    p1_copy(h, d).wait_recv()
+            s = P1[rows_of(h, 0), :]
+            for d in range(1, 8):
+                s = s + PIN[rows_of(h, d), :]
+            rounded = s.astype(jnp.bfloat16).astype(jnp.float32)
+            gap = jnp.sum(jnp.where(lane_h >= 64, s, 0.0), axis=1, keepdims=True)
+            g0 = jax.nn.sigmoid(gap)
+            gated = rounded * jnp.where(lane_h < 32, g0, 1.0 - g0)
+            pair = jnp.where(lane_h < 64, gated, 0.0).astype(jnp.bfloat16)
+            TS[pl.ds(h * half, half), :] = pair
+            TIN[rows_of(h, 0), :] = pair
+            for hh, d in groups:
+                if hh == h:
+                    t_copy(h, d).start()
+
+    def take_gated():
+        for h, d in groups:
+            t_copy(h, d).wait_recv()
+
+        def spread(i, carry):
+            rows = pl.ds(mult(i * CHUNK, CHUNK), CHUNK)
+            c = CODE[rows, :]
+            id0, id1 = c >> 5, c & 31
+            t = TIN[rows, :].astype(jnp.float32)
+            t0 = jnp.where(lane < 32, t, 0.0)
+            t1 = t - t0
+            t0 = t0 + pltpu.roll(t0, 32, 1)
+            t0 = t0 + pltpu.roll(t0, 64, 1)
+            t1 = t1 + pltpu.roll(t1, 32, 1)
+            t1 = t1 + pltpu.roll(t1, 64, 1)
+            for py in range(NY):
+                named = group8 + py
+                part = jnp.where(id0 == named, t0, jnp.where(id1 == named, t1, 0.0))
+                A[rows, py * block : (py + 1) * block] = part.astype(jnp.bfloat16)
+            return carry
+
+        lax.fori_loop(0, total // CHUNK, spread, 0)
+
+    def down_step(s):
+        ring_step(DN, yd_s, yd_r, s)
+
+    def up_step(s):
+        ring_step(UP, yu_s, yu_r, s)
+
+    def up_send():
+        for i in range(1, 4):
+            x_copy(up, UP, xu_s, xu_r, i).start()
+
+    def up_start():
+        x_local(up, UP, xu_r).wait()
+        ring_start(UP, yu_s, yu_r, 0)
+        for i in range(1, 4):
+            x_copy(up, UP, xu_s, xu_r, i).wait_recv()
+            ring_start(UP, yu_s, yu_r, i)
+
+    send_frozen()
+    up_send()
+    take_ids()
+    down_step(1)
+    down_step(2)
+    take_tokens()
     low_rank(y, True)
-    ring_step(DN, yd_s, yd_r, 3)
-    x_local(up, UP, xu_r).wait()
-    ring_start(UP, yu_s, yu_r, 0)
-    for i in range(1, 4):
-        x_copy(up, UP, xu_s, xu_r, i).wait_recv()
-        ring_start(UP, yu_s, yu_r, i)
-    for s in (1, 2):
-        low_rank(lax.rem(y + NY - s, NY))
-        low_rank(lax.rem(y + s, NY))
-    ring_step(DN, yd_s, yd_r, 4)
-    low_rank(lax.rem(y + NY - 3, NY))
-    low_rank(lax.rem(y + 3, NY))
-    low_rank(lax.rem(y + 4, NY))
-
-    def pack(i, carry):
-        rows = pl.ds(mult(i * CHUNK, CHUNK), CHUNK)
-        a0, a1 = ACC0[rows, :], ACC1[rows, :]
-        a0 = a0 + pltpu.roll(a0, 64, 1)
-        a0 = a0 + pltpu.roll(a0, 32, 1)
-        a1 = a1 + pltpu.roll(a1, 64, 1)
-        a1 = a1 + pltpu.roll(a1, 32, 1)
-        low = jnp.where(lane < 32, a0, a1)
-        P1[rows, :] = jnp.where(lane < 64, low, jnp.where(lane < 96, ACCR[rows, :], 0.0))
-        return carry
-
-    lax.fori_loop(0, total // CHUNK, pack, 0)
-
-    def p1_copy(h, d):
-        i = h * 8 + d
-        return remote(P1.at[rows_of(h, d)], PIN.at[rows_of(h, d)], p1_s.at[i], p1_r.at[i], partner(h, d))
-
-    for h, d in groups:
-        p1_copy(h, d).start()
-    ring_step(UP, yu_s, yu_r, 1)
-    for h, d in groups:
-        p1_copy(h, d).wait_recv()
-
-    def t_copy(h, d):
-        i = h * 8 + d
-        return remote(TS.at[pl.ds(h * half, half)], TIN.at[rows_of(h, d)], t_s.at[i], t_r.at[i], partner(h, d))
-
-    lane_h = lax.broadcasted_iota(jnp.int32, (half, 128), 1)
-    for h in range(2):
-        s = P1[rows_of(h, 0), :]
-        for d in range(1, 8):
-            s = s + PIN[rows_of(h, d), :]
-        rounded = s.astype(jnp.bfloat16).astype(jnp.float32)
-        gap = jnp.sum(jnp.where(lane_h >= 64, s, 0.0), axis=1, keepdims=True)
-        g0 = jax.nn.sigmoid(gap)
-        gated = rounded * jnp.where(lane_h < 32, g0, 1.0 - g0)
-        pair = jnp.where(lane_h < 64, gated, 0.0).astype(jnp.bfloat16)
-        TS[pl.ds(h * half, half), :] = pair
-        TIN[rows_of(h, 0), :] = pair
-        for hh, d in groups:
-            if hh == h:
-                t_copy(h, d).start()
-
-    ring_step(UP, yu_s, yu_r, 2)
-    for h, d in groups:
-        t_copy(h, d).wait_recv()
-
-    def spread(i, carry):
-        rows = pl.ds(mult(i * CHUNK, CHUNK), CHUNK)
-        c = CODE[rows, :]
-        id0, id1 = c >> 5, c & 31
-        t = TIN[rows, :].astype(jnp.float32)
-        t0 = jnp.where(lane < 32, t, 0.0)
-        t1 = t - t0
-        t0 = t0 + pltpu.roll(t0, 32, 1)
-        t0 = t0 + pltpu.roll(t0, 64, 1)
-        t1 = t1 + pltpu.roll(t1, 32, 1)
-        t1 = t1 + pltpu.roll(t1, 64, 1)
-        for py in range(NY):
-            named = group8 + py
-            part = jnp.where(id0 == named, t0, jnp.where(id1 == named, t1, 0.0))
-            A[rows, py * block : (py + 1) * block] = part.astype(jnp.bfloat16)
-        return carry
-
-    lax.fori_loop(0, total // CHUNK, spread, 0)
-    ring_step(UP, yu_s, yu_r, 3)
+    low_rank_at(1)
+    down_step(3)
+    up_start()
+    low_rank_at(2)
+    low_rank_at(3)
+    down_step(4)
+    low_rank_at(4)
+    send_partials()
+    up_step(1)
+    send_gated()
+    up_step(2)
+    take_gated()
+    up_step(3)
+    up_step(4)
     for b in range(per_class):
         into = FZ.at[pl.ds(b * fz_rows, fz_rows)]
         pltpu.make_async_copy(frozen, into, fz_r.at[b]).wait()
-    ring_step(UP, yu_s, yu_r, 4)
 
     def rb_copy(h, d):
         i = h * 8 + d
@@ -357,7 +389,7 @@
         lanes = square[:, 0:128]
         for j in range(1, width // 128):
             lanes = lanes + square[:, j * 128 : (j + 1) * 128]
-        scaled = (combined * gain[:, own_cols]).astype(jnp.bfloat16)
+        scaled = (combined * GAIN[...]).astype(jnp.bfloat16)
         PB[rows, 0:features] = jnp.dot(scaled, FZ[...], preferred_element_type=jnp.float32)
         PB[rows, features : features + 128] = lanes
         for k in blocks:
@@ -414,14 +446,14 @@
     dma = pltpu.SemaphoreType.DMA
     any_spec = pl.BlockSpec(memory_space=pltpu.HBM)
     vmem = pl.BlockSpec(memory_space=pltpu.VMEM)
-    sems = [16] * 4 + [4] * 4 + [32] * 4 + [4] * 2 + [16] * 10 + [1]
+    sems = [16] * 4 + [4] * 4 + [32] * 4 + [4] * 2 + [16] * 10 + [2]
     return pl.pallas_call(
         kernel,
         out_shape=(
             jax.ShapeDtypeStruct((rows, width), bf),
             jax.ShapeDtypeStruct((rows, features), bf),
         ),
-        in_specs=[any_spec] * 6 + [vmem],
+        in_specs=[any_spec] * 7,
         out_specs=(any_spec, vmem),
         scratch_shapes=[
             pltpu.VMEM((total, part), bf),
@@ -444,20 +476,26 @@
             pltpu.VMEM((total, features + 128), f32),
             pltpu.VMEM((total, features + 128), bf),
             pltpu.VMEM((total, features + 128), bf),
+            pltpu.VMEM((1, part), f32),
         ]
         + [dma((n,)) for n in sems],
         compiler_params=pltpu.CompilerParams(
-            collective_id=0, has_side_effects=True, vmem_limit_bytes=60 * 1024 * 1024
+            collective_id=0, has_side_effects=True, vmem_limit_bytes=50 * 1024 * 1024
         ),
         cost_estimate=pl.CostEstimate(flops=6_000_000_000, bytes_accessed=20_000_000, transcendentals=0),
     )(
-        tokens,
-        jnp.swapaxes(route_ids, 0, 1),
-        jnp.swapaxes(adapter_down[0], 0, 1),
-        adapter_up[0],
-        jnp.swapaxes(router_weight, 0, 1),
-        frozen_weight,
-        norm_gain[None, :],
+        *[
+            pltpu.with_memory_space_constraint(a, pltpu.HBM)
+            for a in (
+                tokens,
+                jnp.swapaxes(route_ids, 0, 1),
+                jnp.swapaxes(adapter_down[0], 0, 1),
+                adapter_up[0],
+                jnp.swapaxes(router_weight, 0, 1),
+                frozen_weight,
+                norm_gain[None, :],
+            )
+        ]
     )
 
 

time: 103 us -> 91.4 us (0.89)
  the two profiles are of different devices: /device:TPU:128 before, /device:TPU:1 now
where the time goes in v3:
time: 91.4 us; the launch traced here: 91.3 us
  Pallas kernels  88.8 us (97%)
  local copies, waits for them, and re-layouts  1.8 us (2%)
    pallas_call x1, Pallas kernels, shards(): pl.pallas_call(kernel, out_shape=(jax.ShapeDtypeStruct((rows, width), bf)...  88.8 us

profile of v3, /device:TPU:1, one launch (start us, length us, event | category | flops | bytes accessed | tf_op | source)
XLA Modules:
  0.0 91.3 jit_solution(10589459745283087513)
XLA Ops:
  0.6 88.8 %shard_map.86 = (bf16[128,6144]{1,0:T(8,128)(2,1)S(1)}, bf16[128,512]{1,0:T(8,128)(2,1)S(1)}) custom-call(bf16[128,6144]{1,0:T(8,128)(2,1)} %tok.1, s32[2,128]{1,0:T(2,128)} %bitcast.11, bf16[32,6144]{1,0:T(8,128)(2,1)} %bitcast.7, bf16[32,6144]{1,0:T(8,128)(2,1)} %bitcast.8, bf16[32,6144]{1,0:T(8,128)(2,1)} %bitcast.9, bf16[192,512]{1,0:T(8,128)(2,1)} %frozen.1, ...), custom_call_target="tpu_custom_call" | custom-call | flops 6000000000 | bytes 20000000 | tf_op jit(solution)/shard_map/pallas_call | solution.py:450
  89.5 1.1 %copy.11 = bf16[128,6144]{1,0:T(8,128)(2,1)} copy(bf16[128,6144]{1,0:T(8,128)(2,1)S(1)} %get-tuple-element.4) | data formatting | bytes 3145728
  90.6 0.7 copy.12

commit v4 on v3

--- a/solution.py
+++ b/solution.py
@@ -404,15 +404,6 @@
             p2_copy(h, d).start()
 
     for h in range(2):
-        ps_copy(h, 1).wait_recv()
-        s = PB[rows_of(h, 0), :] + PS[rows_of(h, 0), :]
-        for d in (6, 4, 2):
-            p2_copy(h, d).wait_recv()
-            s = s + PIN2[rows_of(h, d), :].astype(jnp.float32)
-        mean = jnp.sum(s[:, features:], axis=1, keepdims=True) / tok.shape[1]
-        proj[pl.ds(h * half, half), :] = (s[:, :features] * lax.rsqrt(mean + 1e-05)).astype(jnp.bfloat16)
-
-    for h in range(2):
         rb_local(h).wait()
     for h, d in groups:
         rb_copy(h, d).wait_recv()
@@ -421,8 +412,6 @@
     for h in range(2):
         for d in (1, 3, 5, 7):
             ps_copy(h, d).wait_send()
-        for d in (2, 4, 6):
-            p2_copy(h, d).wait_send()
     for i in range(1, 4):
         x_copy(down, DN, xd_s, xd_r, i).wait_send()
         x_copy(up, UP, xu_s, xu_r, i).wait_send()
@@ -435,6 +424,19 @@
         @pl.when(fz_other(k))
         def _():
             fz_copy(k).wait_send()
+
+    for h in range(2):
+        ps_copy(h, 1).wait_recv()
+        s = PB[rows_of(h, 0), :] + PS[rows_of(h, 0), :]
+        for d in (6, 4, 2):
+            p2_copy(h, d).wait_recv()
+            s = s + PIN2[rows_of(h, d), :].astype(jnp.float32)
+        mean = jnp.sum(s[:, features:], axis=1, keepdims=True) / tok.shape[1]
+        proj[pl.ds(h * half, half), :] = (s[:, :features] * lax.rsqrt(mean + 1e-05)).astype(jnp.bfloat16)
+
+    for h in range(2):
+        for d in (2, 4, 6):
+            p2_copy(h, d).wait_send()
 
 
 def shards(tokens, route_ids, router_weight, adapter_down, adapter_up, norm_gain, frozen_weight):

time: 91.4 us -> 91.2 us (level)
  no operation moved by 1% of the time
where the time goes in v4:
time: 91.2 us; the launch traced here: 91 us
  Pallas kernels  88.6 us (97%)
  local copies, waits for them, and re-layouts  1.8 us (2%)
    pallas_call x1, Pallas kernels, shards(): pl.pallas_call(kernel, out_shape=(jax.ShapeDtypeStruct((rows, width), bf)...  88.6 us

profile of v4, /device:TPU:1, one launch (start us, length us, event | category | flops | bytes accessed | tf_op | source)
XLA Modules:
  0.0 91.0 jit_solution(10792219541468259671)
XLA Ops:
  0.6 88.6 %shard_map.86 = (bf16[128,6144]{1,0:T(8,128)(2,1)S(1)}, bf16[128,512]{1,0:T(8,128)(2,1)S(1)}) custom-call(bf16[128,6144]{1,0:T(8,128)(2,1)} %tok.1, s32[2,128]{1,0:T(2,128)} %bitcast.11, bf16[32,6144]{1,0:T(8,128)(2,1)} %bitcast.7, bf16[32,6144]{1,0:T(8,128)(2,1)} %bitcast.8, bf16[32,6144]{1,0:T(8,128)(2,1)} %bitcast.9, bf16[192,512]{1,0:T(8,128)(2,1)} %frozen.1, ...), custom_call_target="tpu_custom_call" | custom-call | flops 6000000000 | bytes 20000000 | tf_op jit(solution)/shard_map/pallas_call | solution.py:452
  89.2 1.1 %copy.11 = bf16[128,6144]{1,0:T(8,128)(2,1)} copy(bf16[128,6144]{1,0:T(8,128)(2,1)S(1)} %get-tuple-element.4) | data formatting | bytes 3145728
  90.4 0.7 copy.12
